TPU v7x, 256 devices: a whole 4x4x8 slice. The times are simulated.
256 devices in a mesh: grp: 32 (over x, y, core), tp: 8 (over z).
Axes of the slice: x: 4, y: 4, z: 8, core: 2. Of those that a mesh axis runs over, the one named last changes fastest.
Arguments:
- queries: bfloat16 [32, 128, 8192], P('grp', None, 'tp'), may hold values from -10.5 to 10.5
- span_kv: bfloat16 [32, 128, 8, 256], P('grp', None, 'tp'), may hold values from -6 to 6
- cache: bfloat16 [1536, 128, 8, 256], P('grp', None, 'tp'), may hold values from -6 to 6
- block_owner: int32 [1536, 1], P('grp'), may hold values from 0 to 31; in each aligned block of 48 rows (0 to 47, 48 to 95, ...) at most 2 rows name the same one
- block_fill: int32 [1536, 1], P('grp'), may hold values from 1 to 128
- out_weight: bfloat16 [8192, 8192], P('tp', 'grp'), may hold values from -0.25 to 0.25
Outputs:
- attn_out: bfloat16 [4096, 8192], P('tp', 'grp')
Inputs may be any that keep to these rules, and one draw needn't show every extreme that they name: `block_owner`: among the 48 blocks stored on one group (rows g * 48 to g * 48 + 47) no response is named more than 2 times; every response owns at least one block.
All inputs are finite; a program needn't handle non-finite values.
Results may differ from a plain program's by a relative error of at most 0.022.
Values may be sent and summed in bfloat16 or wider, within the bound.
A program may use at most 128 MiB of HBM per device.

v0:
```python
import jax
import jax.numpy as jnp
from jax import lax
from jax.sharding import PartitionSpec as P

KB = 128
CAP = 2


def body(queries, span_kv, cache, block_owner, block_fill, out_weight):
    groups = lax.axis_size("grp")
    slots = cache.shape[0]
    kv_local = cache.shape[2]
    head_size = cache.shape[3] // 2
    new_rows = queries.shape[1]
    q_width = queries.shape[2]
    per_kv = q_width // (kv_local * head_size)
    owners = block_owner[:, 0]
    fills = block_fill[:, 0]
    one_hot = (owners[:, None] == jnp.arange(groups, dtype=jnp.int32)[None, :]).astype(jnp.int32)
    local_rank = jnp.sum((jnp.cumsum(one_hot, 0) - one_hot) * one_hot, 1)
    target = owners * CAP + local_rank
    matches = jnp.arange(groups * CAP, dtype=jnp.int32)[:, None] == target[None, :]
    packed = jnp.dot(
        matches.astype(jnp.bfloat16), cache.reshape(slots, -1), preferred_element_type=jnp.float32
    )
    packed = packed.astype(jnp.bfloat16).reshape(groups, CAP * KB, kv_local, 2 * head_size)
    sent_fill = jnp.sum(jnp.where(matches, fills[None, :], 0), 1).reshape(groups, CAP)
    arrived, arrived_fill = (
        lax.all_to_all(packed, "grp", split_axis=0, concat_axis=0, tiled=True),
        lax.all_to_all(sent_fill, "grp", split_axis=0, concat_axis=0, tiled=True),
    )
    seen = (jnp.arange(KB, dtype=jnp.int32)[None, None, :] < arrived_fill[:, :, None]).reshape(-1)
    prefix_keys = seen.shape[0]
    causal = jnp.arange(new_rows)[None, :] <= jnp.arange(new_rows)[:, None]
    mask = jnp.concatenate([jnp.broadcast_to(seen[None, :], (new_rows, prefix_keys)), causal], 1)
    every = jnp.concatenate([arrived.reshape(prefix_keys, kv_local, 2 * head_size), span_kv[0]], 0)
    query = queries[0].reshape(new_rows, kv_local, per_kv, head_size)
    scores = jnp.einsum(
        "cjgd,njd->jgcn", query, every[:, :, :head_size], preferred_element_type=jnp.float32
    )
    scores = jnp.where(mask[None, None], scores * (1.0 / head_size**0.5), -1e30)
    top = jnp.max(scores, -1, keepdims=True)
    expo = jnp.exp(scores - top)
    weights = (expo / jnp.sum(expo, -1, keepdims=True)).astype(jnp.bfloat16)
    heads = jnp.einsum(
        "jgcn,njd->cjgd", weights, every[:, :, head_size:], preferred_element_type=jnp.float32
    )
    heads_out = heads.astype(jnp.bfloat16).reshape(1, new_rows, q_width)
    terms = jnp.dot(
        lax.all_gather(heads_out, "grp", axis=0, tiled=True).reshape(-1, q_width),
        out_weight,
        preferred_element_type=jnp.float32,
    )
    summed = lax.psum_scatter(terms.astype(jnp.bfloat16), "tp", scatter_dimension=0, tiled=True)
    return summed


def solution(mesh):
    in_specs = (
        P("grp", None, "tp"),
        P("grp", None, "tp", None),
        P("grp", None, "tp", None),
        P("grp", None),
        P("grp", None),
        P("tp", "grp"),
    )
    out_specs = P("tp", "grp")
    return jax.shard_map(body, mesh=mesh, in_specs=in_specs, out_specs=out_specs, check_vma=False)
```

profile of v0, /device:TPU:1, one launch (start us, length us, event | category | flops | bytes accessed | tf_op | source)
XLA Modules:
  0.0 251.7 jit_solution(13098153814974488039)
XLA Ops:
  6.5 0.8 fusion.17
  7.3 0.1 reduce_window_sum.11
  7.4 0.8 select_reduce_fusion.1
  8.2 0.7 multiply_add_fusion
  8.9 0.7 select_reduce_fusion
  9.6 0.7 all_to_all.10
  10.4 8.6 %all-to-all-start.1 = ((s32[32,1,2]{2,1,0:T(1,128)}), s32[32,1,2]{2,1,0:T(1,128)S(1)}, u32[]{:S(2)}, u32[]{:S(2)}) async-start(s32[32,1,2]{2,1,0:T(1,128)} %bitcast.7), calls=%async_computation.1 | async-start | bytes 32768 | tf_op jit(solution)/shard_map/all_to_all | solution.py:31
  19.0 3.8 %copy.38 = bf16[6,8,128,256]{3,1,2,0:T(8,128)(2,1)S(1)} copy(bf16[6,8,128,256]{3,2,1,0:T(8,128)(2,1)} %bitcast.59) | data formatting | bytes 6291456
  22.7 3.3 %convolution_convert_fusion = bf16[64,32768]{1,0:T(8,128)(2,1)} fusion(bf16[48,32768]{1,0:T(8,128)(2,1)S(1)} %bitcast.58, s32[48]{0:T(128)S(1)} %multiply_add_fusion), kind=kOutput, calls=%fused_computation | convolution fusion | flops 203426816 | bytes 7340224 | tf_op jit(solution)/shard_map/dot_general | solution.py:24
  26.1 7.4 %reshape.76 = bf16[32,256,1,256]{3,1,0,2:T(8,128)(2,1)} reshape(bf16[64,32768]{1,0:T(8,128)(2,1)} %convolution_convert_fusion) | data formatting | bytes 8388608 | tf_op jit(solution)/shard_map/reshape | solution.py:27
  33.5 7.6 %all-to-all-start = ((bf16[32,256,1,256]{3,1,2,0:T(8,128)(2,1)}), bf16[32,256,1,256]{3,1,2,0:T(8,128)(2,1)}, u32[]{:S(2)}, u32[]{:S(2)}) async-start(bf16[32,256,1,256]{3,1,2,0:T(8,128)(2,1)} %bitcast.57), calls=%async_computation | async-start | bytes 8388608 | tf_op jit(solution)/shard_map/all_to_all | solution.py:30
  41.1 0.2 all-gather.2.cloned.1.call-start
  41.4 0.1 iota_compare_fusion.1
  41.5 8.3 %pad_add_fusion = pred[128,8320]{0,1:T(8,128)(4,1)S(1)} fusion(pred[128,128]{0,1:T(8,128)(4,1)S(1)} %iota_compare_fusion, pred[8320]{0:T(1024)(128)(4,1)S(1)} %pad.clone), kind=kLoop, calls=%fused_computation.11 | loop fusion | flops 1064960 | bytes 1089664 | tf_op jit(solution)/shard_map/concatenate | solution.py:36
  49.9 43.4 %all-to-all-done = bf16[32,256,1,256]{3,1,2,0:T(8,128)(2,1)} async-done(((bf16[32,256,1,256]{3,1,2,0:T(8,128)(2,1)}), bf16[32,256,1,256]{3,1,2,0:T(8,128)(2,1)}, u32[]{:S(2)}, u32[]{:S(2)}) %all-to-all-start) | async-done | bytes 4194336 | tf_op jit(solution)/shard_map/all_to_all | solution.py:30
  93.3 14.9 %fusion.1 = (f32[8,128]{1,0:T(8,128)S(1)}, f32[8320,128,8]{1,0,2:T(8,128)}) fusion(pred[128,8320]{0,1:T(8,128)(4,1)S(1)} %pad_add_fusion, bf16[128,8,128]{2,1,0:T(8,128)(2,1)S(1)} %bitcast.61, bf16[128,1,256]{2,0,1:T(8,128)(2,1)S(1)} %bitcast.67, bf16[8192,1,256]{2,0,1:T(8,128)(2,1)} %bitcast.2), kind=kOutput, calls=%fused_computation.5 | convolution fusion | flops 2210855936 | bytes 39669760 | tf_op jit(solution)/shard_map/cjgd,njd->jgcn/dot_general | solution.py:39
  108.2 14.4 %fusion = f32[8,128]{1,0:T(8,128)S(1)} fusion(f32[8320,128,8]{1,0,2:T(8,128)} %get-tuple-element.6, f32[8,128]{1,0:T(8,128)S(1)} %get-tuple-element.5, pred[128,8320]{0,1:T(8,128)(4,1)S(1)} %pad_add_fusion), kind=kLoop, calls=%fused_computation.4 | loop fusion | flops 34077696 | bytes 35151872 | tf_op jit(solution)/shard_map/reduce_sum | solution.py:45
  122.5 16.1 %fusion.11 = bf16[128,8,128]{2,0,1:T(8,128)(2,1)S(1)} fusion(f32[8,128]{1,0:T(8,128)S(1)} %fusion, f32[8,128]{1,0:T(8,128)S(1)} %get-tuple-element.5, f32[8320,128,8]{1,0,2:T(8,128)} %get-tuple-element.6, pred[128,8320]{0,1:T(8,128)(4,1)S(1)} %pad_add_fusion, bf16[8192,1,256]{2,0,1:T(8,128)(2,1)} %bitcast.2, bf16[128,1,256]{2,0,1:T(8,128)(2,1)S(1)} %bitcast.68), kind=kOutput, calls=%fused_computation.18 | convolution fusion | flops 2228027392 | bytes 39673856 | tf_op jit(solution)/shard_map/jgcn,njd->cjgd/dot_general | solution.py:46
  138.6 0.8 copy.33
  139.5 0.0 all-gather.2.cloned.1.call-update
  139.5 0.0 reduce-scatter.2.cloned.1.call-start
  139.5 60.8 %all-gather.2.cloned.1.call-done = bf16[32,128,1024]{2,1,0:T(8,128)(2,1)} async-done(((bf16[1,128,1024]{2,1,0:T(8,128)(2,1)}), bf16[32,128,1024]{2,1,0:T(8,128)(2,1)}) %all-gather.2.cloned.1.call-update) | async-done | bytes 8388624 | tf_op jit(solution)/shard_map/all_gather | solution.py:51
  200.3 7.1 %convolution_convert_fusion.1 = bf16[4096,256]{1,0:T(8,128)(2,1)} fusion(bf16[4096,1024]{1,0:T(8,128)(2,1)} %bitcast.66, bf16[1024,256]{1,0:T(8,128)(2,1)S(1)} %copy-done), kind=kOutput, calls=%fused_computation.8 | convolution fusion | flops 2148532224 | bytes 11010048 | tf_op jit(solution)/shard_map/dot_general | solution.py:50
  207.5 37.4 %reduce-scatter.2.cloned.1.call-done = bf16[512,256]{1,0:T(8,128)(2,1)} async-done(((bf16[4096,256]{1,0:T(8,128)(2,1)}), bf16[512,256]{1,0:T(8,128)(2,1)}) %reduce-scatter.2.cloned.1.call-update) | async-done | bytes 262160 | tf_op jit(solution)/shard_map/reduce_scatter | solution.py:55
  (12 shorter events, 0.1 us)
Async XLA Ops:
  6.5 193.8 %copy-start = (bf16[1024,256]{1,0:T(8,128)(2,1)S(1)}, bf16[1024,256]{1,0:T(8,128)(2,1)}, u32[]{:S(2)}) copy-start(bf16[1024,256]{1,0:T(8,128)(2,1)} %param.11) | copy-start | bytes 1572868
  10.4 23.1 %all-to-all-start.1 = ((s32[32,1,2]{2,1,0:T(1,128)}), s32[32,1,2]{2,1,0:T(1,128)S(1)}, u32[]{:S(2)}, u32[]{:S(2)}) async-start(s32[32,1,2]{2,1,0:T(1,128)} %bitcast.7), calls=%async_computation.1 | async-start | bytes 32768 | tf_op jit(solution)/shard_map/all_to_all | solution.py:31
  33.5 7.8 %copy-start.1 = (bf16[1,128,1024]{2,1,0:T(8,128)(2,1)S(1)}, bf16[1,128,1024]{2,1,0:T(8,128)(2,1)}, u32[]{:S(2)}) copy-start(bf16[1,128,1024]{2,1,0:T(8,128)(2,1)} %param.6) | copy-start | bytes 786436
  33.5 59.8 %copy-start.2 = (bf16[1,128,1,256]{3,1,2,0:T(8,128)(2,1)S(1)}, bf16[1,128,1,256]{3,1,2,0:T(8,128)(2,1)}, u32[]{:S(2)}) copy-start(bf16[1,128,1,256]{3,1,2,0:T(8,128)(2,1)} %param.7) | copy-start | bytes 196612
  33.5 59.8 %all-to-all-start = ((bf16[32,256,1,256]{3,1,2,0:T(8,128)(2,1)}), bf16[32,256,1,256]{3,1,2,0:T(8,128)(2,1)}, u32[]{:S(2)}, u32[]{:S(2)}) async-start(bf16[32,256,1,256]{3,1,2,0:T(8,128)(2,1)} %bitcast.57), calls=%async_computation | async-start | bytes 8388608 | tf_op jit(solution)/shard_map/all_to_all | solution.py:30
  41.1 159.2 %all-gather.2.cloned.1.call-start = ((), (), s32[]{:S(2)}) async-start(), calls=%async_computation.3 | async-start | bytes 8650752 | tf_op jit(solution)/shard_map/all_gather | solution.py:51
  139.5 105.4 %reduce-scatter.2.cloned.1.call-start = ((), (), s32[]{:S(2)}) async-start(), calls=%async_computation.4 | async-start | bytes 2359296 | tf_op jit(solution)/shard_map/reduce_scatter | solution.py:55
Sparse Core Ops, SparseCore 0:
  139.6 60.6 all-gather.1
  207.6 37.2 reduce-scatter.1
where the time goes:
time: 255 us; the launch traced here: 252 us
  waiting for transfers between devices  142 us (56%)
  matrix products  41.4 us (16%)
  other arithmetic  25.9 us (10%)
  starting transfers between devices  16.4 us (6%)
  between operations  13.5 us (5%)
  local copies, waits for them, and re-layouts  12.8 us (5%)
    all_gather x1, waiting for transfers between devices, body(): lax.all_gather(heads_out, 'grp', axis=0, tiled=True).reshape(-1, q_width)  60.8 us
    all_to_all x1, waiting for transfers between devices, body(): lax.all_to_all(packed, 'grp', split_axis=0, concat_axis=0, tiled=True)  43.4 us
    reduce_scatter x1, waiting for transfers between devices, body(): lax.psum_scatter(terms.astype(jnp.bfloat16), 'tp', scatter_dimension=0, t...  37.4 us
    dot_general x1, matrix products, body(): jnp.einsum('jgcn,njd->cjgd', weights, every[:, :, head_size:], preferred_...  16.1 us
    dot_general x1, matrix products, body(): jnp.einsum('cjgd,njd->jgcn', query, every[:, :, :head_size], preferred_el...  14.9 us
    reduce_sum x1, other arithmetic, body(): weights = (expo / jnp.sum(expo, -1, keepdims=True)).astype(jnp.bfloat16)  14.4 us
    all_to_all x1, starting transfers between devices, body(): lax.all_to_all(sent_fill, 'grp', split_axis=0, concat_axis=0, tiled=True)  8.59 us
    concatenate x1, other arithmetic, body(): jnp.concatenate([jnp.broadcast_to(seen[None, :], (new_rows, prefix_keys))...  8.32 us
  transfers between devices with their start and end apart: 4, of which 3 were waited for; matrix products, arithmetic and copies ran while one was open for 9% of the time, Pallas kernels for 0%

commit v1 on v0

v1 whole, which is shorter than its diff:
```python
import functools

import jax
import jax.numpy as jnp
from jax import lax
from jax.experimental import pallas as pl
from jax.experimental.pallas import tpu as pltpu
from jax.sharding import PartitionSpec as P

MESH = pl.DeviceIdType.MESH
NX, NY, NC, NZ = 4, 4, 2, 8
GRP = NX * NY * NC
CAP = 2
KB = 128
HD = 128
NEW = 128
WIDTH = 1024
FEAT = 256
CHUNK = NEW // NZ
NEG = -1e30
LOG2E = 1.4426950408889634
F32 = jnp.float32
BF16 = jnp.bfloat16
ORDER = ((0, 0), (3, 0), (1, 0), (0, 3), (0, 1), (2, 0), (3, 3), (3, 1), (1, 3), (1, 1), (0, 2), (2, 3), (2, 1), (3, 2), (1, 2), (2, 2))


def table_kernel(owner_ref, fill_ref, table_ref, count_ref):
    slots = owner_ref.shape[0]

    def clear(i, c):
        count_ref[i] = 0
        table_ref[2 * i] = 0
        table_ref[2 * i + 1] = 0
        table_ref[2 * GRP + i] = 0
        return c

    lax.fori_loop(0, GRP, clear, 0)

    def place(b, c):
        own = owner_ref[b]
        rank = count_ref[own]
        count_ref[own] = rank + 1
        table_ref[2 * own + rank] = b
        fill = fill_ref[b]
        held = table_ref[2 * GRP + own]
        table_ref[2 * GRP + own] = held + jnp.where(rank == 0, fill, fill * 256)
        return c

    lax.fori_loop(0, slots, place, 0)


def main_kernel(
    table, q_ref, span_ref, cache_ref, w_ref, o_ref,
    send, sfill, recv, rfill, qs, m, acc, wfull, heads, gath, total, zout, obuf,
    kv_s, kv_r, f_s, f_r, w_s, w_r, a_s, a_r, g_s, g_r, b_s, b_r, o_s, o_r,
):
    g = lax.axis_index("grp")
    t = lax.axis_index("tp")
    x, y, c = g // (NY * NC), (g // NC) % NY, g % NC

    def at(px, py, pc):
        return (px % NX) * (NY * NC) + (py % NY) * NC + pc

    sib = at(x, y, 1 - c)

    def copy(src, dst, ssem, rsem, dev):
        return pltpu.make_async_remote_copy(
            src_ref=src, dst_ref=dst, send_sem=ssem, recv_sem=rsem, device_id=dev, device_id_type=MESH
        )

    barrier = pltpu.get_barrier_semaphore()

    def greet(s, k):
        pl.semaphore_signal(barrier, inc=1, device_id=((g + s) % GRP, t), device_id_type=MESH)
        return k

    lax.fori_loop(1, GRP, greet, 0)
    for s in range(1, NZ):
        pl.semaphore_signal(barrier, inc=1, device_id=(g, (t + s) % NZ), device_id_type=MESH)
    pl.semaphore_wait(barrier, GRP - 1 + NZ - 1)

    up, down = (t + 1) % NZ, (t + NZ - 1) % NZ
    wfull[t] = w_ref[...]
    half = WIDTH // 2

    def wcopy(n, z, lo, size, k, dev):
        part = wfull.at[z, pl.ds(lo, size)]
        return copy(part, part, w_s.at[n], w_r.at[z, k], (g, dev))

    wsends = [wcopy(0, t, 0, WIDTH, 0, up), wcopy(1, t, 0, WIDTH, 0, down)]
    for d in wsends:
        d.start()

    def wpass(j, lo, hi):
        low, high = (t + NZ - j) % NZ, (t + j) % NZ
        wcopy(0, low, 0, WIDTH, 0, up).wait_recv()
        d0 = wcopy(2 * j, low, lo, hi, 0, up)
        d0.start()
        wcopy(0, high, 0, WIDTH, 0, down).wait_recv()
        d1 = wcopy(2 * j + 1, high, half if hi < WIDTH else 0, hi, 1 if hi < WIDTH else 0, down)
        d1.start()
        wsends.extend([d0, d1])

    def where_to(s):
        o = (s * 11) % GRP
        return o // (NY * NC), (o // NC) % NY, o % NC

    def load(dst):
        first = cache_ref[table[2 * dst]]
        second = cache_ref[table[2 * dst + 1]]
        fills = jnp.full((1, KB), table[2 * GRP + dst], jnp.int32)
        return first, second, fills

    def kv_copy(dst, s):
        return copy(send.at[dst], recv.at[g], kv_s.at[s], kv_r.at[g], (dst, t))

    def fill_copy(dst, s):
        return copy(sfill.at[dst], rfill.at[g], f_s.at[s], f_r.at[g], (dst, t))

    def give(s, k):
        dx, dy, dc = where_to(s)
        dst = at(x + dx, y + dy, (c + dc) % NC)
        first, second, fills = load(dst)
        send[dst, :KB] = first
        send[dst, KB:] = second
        sfill[dst] = fills
        kv_copy(dst, s).start()
        fill_copy(dst, s).start()
        return k

    lax.fori_loop(1, GRP, give, 0)
    first, second, fills = load(g)
    recv[g, :KB] = first
    recv[g, KB:] = second
    rfill[g] = fills

    heads_n = WIDTH // HD
    for h in range(heads_n):
        qs[h * NEW:(h + 1) * NEW, :] = q_ref[:, h * HD:(h + 1) * HD]
    factor = LOG2E / HD**0.5
    blk = 256
    ones = jnp.ones((CAP * KB, HD), BF16)

    def scores(rows, keys):
        return lax.dot_general(qs[rows, :], keys, (((1,), (1,)), ((), ())), preferred_element_type=F32) * factor

    span_k, span_v = span_ref[:, :HD], span_ref[:, HD:]
    span_aug = jnp.concatenate([span_v, ones[:NEW]], 1)
    row = lax.broadcasted_iota(jnp.int32, (blk, NEW), 0) % NEW
    col = lax.broadcasted_iota(jnp.int32, (blk, NEW), 1)
    for qb in range(WIDTH // blk):
        rows = pl.ds(qb * blk, blk)
        s = jnp.where(col <= row, scores(rows, span_k), NEG)
        top = jnp.max(s, 1, keepdims=True)
        m[rows, :] = jnp.broadcast_to(top, (blk, HD))
        p = jnp.exp2(s - top).astype(BF16)
        acc[rows, :] = jnp.dot(p, span_aug, preferred_element_type=F32)

    lane = lax.broadcasted_iota(jnp.int32, (1, KB), 1)

    def attend(src):
        fills = rfill[src]
        bias = jnp.concatenate(
            [jnp.where(lane < fills % 256, 0.0, NEG), jnp.where(lane < fills // 256, 0.0, NEG)], 1
        )
        keys = recv[src, :, :HD]
        vals = jnp.concatenate([recv[src, :, HD:], ones], 1)
        for qb in range(WIDTH // blk):
            rows = pl.ds(qb * blk, blk)
            s = scores(rows, keys) + bias
            old = m[rows, :]
            new = jnp.maximum(old, jnp.max(s, 1, keepdims=True))
            alpha = jnp.exp2(old - new)
            p = jnp.exp2(s - jnp.concatenate([new, new], 1)).astype(BF16)
            part = jnp.dot(p, vals, preferred_element_type=F32)
            acc[rows, :] = acc[rows, :] * jnp.concatenate([alpha, alpha], 1) + part
            m[rows, :] = new

    attend(g)

    def take(s, k):
        dx, dy, dc = where_to(s)
        src = at(x + NX - dx, y + NY - dy, (c + dc) % NC)
        copy(send.at[src], recv.at[src], kv_s.at[s], kv_r.at[src], (src, t)).wait_recv()
        copy(sfill.at[src], rfill.at[src], f_s.at[s], f_r.at[src], (src, t)).wait_recv()
        attend(src)
        return k

    lax.fori_loop(1, 9, take, 0)
    wpass(1, 0, WIDTH)
    lax.fori_loop(9, 17, take, 0)
    wpass(2, 0, WIDTH)
    lax.fori_loop(17, 25, take, 0)
    wpass(3, 0, half)
    total[...] = jnp.zeros_like(total)
    lax.fori_loop(25, GRP, take, 0)

    for h in range(heads_n):
        rows = pl.ds(h * NEW, NEW)
        out = (acc[rows, :HD] / acc[rows, HD:]).astype(BF16)
        heads[:, :, h * HD:(h + 1) * HD] = out.reshape(NZ, CHUNK, HD)

    def spread(s, k):
        z = (t + s) % NZ
        copy(heads.at[z], gath.at[g, t], a_s.at[s], a_r.at[t], (g, z)).start()
        return k

    lax.fori_loop(1, NZ, spread, 0)
    gath[g, t] = heads[t]

    def spread_in(s, k):
        z = (t + s) % NZ
        copy(heads.at[z], gath.at[g, z], a_s.at[s], a_r.at[z], (g, z)).wait_recv()
        return k

    lax.fori_loop(1, NZ, spread_in, 0)

    sends = []

    def piece(owner, lo, size):
        return gath.at[owner, pl.ds(lo, size)]

    def push(owner, lo, size, quarter, dev):
        part = piece(owner, lo, size)
        d = copy(part, part, g_s.at[len(sends)], g_r.at[owner, quarter], (dev, t))
        d.start()
        sends.append(d)

    def arrived(owner, lo, size, quarter):
        part = piece(owner, lo, size)
        copy(part, part, g_s.at[0], g_r.at[owner, quarter], (sib, t)).wait_recv()

    def place(h, d1, d2, pc):
        return at(x + d1, y + d2, pc) if h == 0 else at(x + d2, y + d1, pc)

    def share(h, owner):
        part = piece(owner, 4 * h, 4)
        d = copy(part, part, b_s.at[len(shared)], b_r.at[owner, h], (sib, t))
        d.start()
        shared.append(d)

    shared = []

    def event(h, d1, d2):
        owner = place(h, d1, d2, c)
        lo = 4 * h
        q = 2 * h
        fwd1, back1 = place(h, 1, 0, c), place(h, 3, 0, c)
        fwd2, back2 = place(h, 0, 1, c), place(h, 0, 3, c)
        last = d2 if d2 else d1
        if last == 2:
            arrived(owner, lo, 2, q)
            arrived(owner, lo + 2, 2, q + 1)
        elif last:
            arrived(owner, lo, 4, q)
        if d2 == 0:
            if d1 == 0:
                push(owner, lo, 4, q, fwd1)
                push(owner, lo, 4, q, back1)
            elif d1 == 3:
                push(owner, lo, 2, q, fwd1)
            elif d1 == 1:
                push(owner, lo + 2, 2, q + 1, back1)
            push(owner, lo, 4, q, fwd2)
            push(owner, lo, 4, q, back2)
        elif d2 == 3:
            push(owner, lo, 2, q, fwd2)
        elif d2 == 1:
            push(owner, lo + 2, 2, q + 1, back2)
        share(h, owner)

    def multiply(h, d2):
        owners = [place(h, d1, d2, pc) for d1 in range(4) for pc in range(2)]
        for d1 in range(4):
            other = place(h, d1, d2, 1 - c)
            part = piece(other, 4 * h, 4)
            copy(part, part, b_s.at[0], b_r.at[other, h], (sib, t)).wait_recv()

        def step(k, sum_):
            z = 4 * h + k
            rows = jnp.concatenate([gath[o, z] for o in owners], 0)
            return sum_ + jnp.dot(rows, wfull[z], preferred_element_type=F32)

        got = lax.fori_loop(0, 4, step, jnp.zeros((len(owners) * CHUNK, FEAT), F32))
        for i, o in enumerate(owners):
            total[o] = total[o] + got[i * CHUNK:(i + 1) * CHUNK]

    for n, (d1, d2) in enumerate(ORDER):
        for h in range(2):
            event(h, d1, d2)
        if n == 0:
            opposite = (t + 4) % NZ
            wcopy(0, opposite, 0, half, 0, up).wait_recv()
            wcopy(0, opposite, half, half, 1, down).wait_recv()
        done = {6: 0, 12: 3, 13: 1, 15: 2}.get(n)
        if done is not None:
            for h in range(2):
                multiply(h, done)

    zout[...] = total[...].astype(BF16)
    per = GRP // NZ

    def ocopy(s):
        z = (t + s) % NZ
        return copy(zout.at[pl.ds(z * per, per)], obuf.at[:, t], o_s.at[s], o_r.at[t], (g, z))

    def hand(s, k):
        ocopy(s).start()
        return k

    lax.fori_loop(1, NZ, hand, 0)
    obuf[:, t] = zout[pl.ds(t * per, per)]

    def hand_in(s, k):
        z = (t + s) % NZ
        copy(zout.at[pl.ds(z * per, per)], obuf.at[:, z], o_s.at[s], o_r.at[z], (g, z)).wait_recv()
        return k

    lax.fori_loop(1, NZ, hand_in, 0)
    o_ref[...] = obuf[...]

    def sent(s, k):
        dx, dy, dc = where_to(s)
        dst = at(x + dx, y + dy, (c + dc) % NC)
        kv_copy(dst, s).wait_send()
        fill_copy(dst, s).wait_send()
        return k

    lax.fori_loop(1, GRP, sent, 0)

    def sent_z(s, k):
        z = (t + s) % NZ
        copy(heads.at[z], gath.at[g, t], a_s.at[s], a_r.at[t], (g, z)).wait_send()
        ocopy(s).wait_send()
        return k

    lax.fori_loop(1, NZ, sent_z, 0)
    for d in wsends + sends + shared:
        d.wait_send()


def body(queries, span_kv, cache, block_owner, block_fill, out_weight):
    slots = cache.shape[0]
    smem = pl.BlockSpec(memory_space=pltpu.SMEM)
    vmem = pl.BlockSpec(memory_space=pltpu.VMEM)
    table = pl.pallas_call(
        table_kernel,
        out_shape=jax.ShapeDtypeStruct((3 * GRP,), jnp.int32),
        in_specs=[smem, smem],
        out_specs=smem,
        scratch_shapes=[pltpu.SMEM((GRP,), jnp.int32)],
    )(block_owner.reshape(slots), block_fill.reshape(slots))
    dma = pltpu.SemaphoreType.DMA
    out = pl.pallas_call(
        main_kernel,
        out_shape=jax.ShapeDtypeStruct((GRP // NZ, NZ, CHUNK, FEAT), BF16),
        in_specs=[smem, vmem, vmem, vmem, vmem],
        out_specs=vmem,
        scratch_shapes=[
            pltpu.VMEM((GRP, CAP * KB, 2 * HD), BF16),
            pltpu.VMEM((GRP, 1, KB), jnp.int32),
            pltpu.VMEM((GRP, CAP * KB, 2 * HD), BF16),
            pltpu.VMEM((GRP, 1, KB), jnp.int32),
            pltpu.VMEM((WIDTH, HD), BF16),
            pltpu.VMEM((WIDTH, HD), F32),
            pltpu.VMEM((WIDTH, 2 * HD), F32),
            pltpu.VMEM((NZ, WIDTH, FEAT), BF16),
            pltpu.VMEM((NZ, CHUNK, WIDTH), BF16),
            pltpu.VMEM((GRP, NZ, CHUNK, WIDTH), BF16),
            pltpu.VMEM((GRP, CHUNK, FEAT), F32),
            pltpu.VMEM((GRP, CHUNK, FEAT), BF16),
            pltpu.VMEM((GRP // NZ, NZ, CHUNK, FEAT), BF16),
            dma((GRP,)), dma((GRP,)), dma((GRP,)), dma((GRP,)),
            dma((NZ,)), dma((NZ, 2)),
            dma((NZ,)), dma((NZ,)),
            dma((40,)), dma((GRP, 4)),
            dma((32,)), dma((GRP, 2)),
            dma((NZ,)), dma((NZ,)),
        ],
        compiler_params=pltpu.CompilerParams(
            collective_id=0, has_side_effects=True, vmem_limit_bytes=50 * 1024 * 1024
        ),
    )(
        table,
        queries.reshape(NEW, WIDTH),
        span_kv.reshape(NEW, 2 * HD),
        cache.reshape(slots, KB, 2 * HD),
        out_weight,
    )
    return out.reshape(GRP // NZ * NEW, FEAT)


def solution(mesh):
    in_specs = (
        P("grp", None, "tp"),
        P("grp", None, "tp", None),
        P("grp", None, "tp", None),
        P("grp", None),
        P("grp", None),
        P("tp", "grp"),
    )
    out_specs = P("tp", "grp")
    return jax.shard_map(body, mesh=mesh, in_specs=in_specs, out_specs=out_specs, check_vma=False)
```

time: 255 us -> 130 us (0.51); the launches traced: 252 us -> 130 us
  waiting for transfers between devices: 142 us -> 0 us
  Pallas kernels: 0 us -> 126 us
  matrix products: 41.4 us -> 0 us
  other arithmetic: 25.9 us -> 0 us
  starting transfers between devices: 16.4 us -> 0 us
  between operations: 13.5 us -> 0.03 us
  local copies, waits for them, and re-layouts: 12.8 us -> 4.19 us
    pallas_call x0 -> x2, Pallas kernels: none -> 126 us  [the longest x1 124 us: body(): pl.pallas_call(main_kernel, out_shape=jax.ShapeDtypeStruct((GRP // NZ, NZ...]
    all_gather x1 -> x0, waiting for transfers between devices: 60.8 us -> none  [body(): lax.all_gather(heads_out, 'grp', axis=0, tiled=True).reshape(-1, q_width)]
    all_to_all x2 -> x0, waiting for transfers between devices: 43.4 us -> none  [the longest x1 43.4 us: body(): lax.all_to_all(packed, 'grp', split_axis=0, concat_axis=0, tiled=True)]
    dot_general x4 -> x0, matrix products: 41.4 us -> none  [the longest x1 16.1 us: body(): jnp.einsum('jgcn,njd->cjgd', weights, every[:, :, head_size:], preferred_...]
    reduce_scatter x1 -> x0, waiting for transfers between devices: 37.4 us -> none  [body(): lax.psum_scatter(terms.astype(jnp.bfloat16), 'tp', scatter_dimension=0, t...]
    all_to_all x2 -> x0, starting transfers between devices: 16.2 us -> none  [the longest x1 8.59 us: body(): lax.all_to_all(sent_fill, 'grp', split_axis=0, concat_axis=0, tiled=True)]
    reduce_sum x3 -> x0, other arithmetic: 16 us -> none  [the longest x1 14.4 us: body(): weights = (expo / jnp.sum(expo, -1, keepdims=True)).astype(jnp.bfloat16)]
    concatenate x1 -> x0, other arithmetic: 8.32 us -> none  [body(): jnp.concatenate([jnp.broadcast_to(seen[None, :], (new_rows, prefix_keys))...]
  transfers between devices with their start and end apart: 4 -> 0, of which waited for: 3 -> 0; matrix products, arithmetic and copies ran while one was open for 9% -> 0% of each run, Pallas kernels for 0% -> 0%
where the time goes in v1:
time: 130 us
  Pallas kernels  126 us (97%)
  local copies, waits for them, and re-layouts  4.19 us (3%)
    pallas_call x1, Pallas kernels, body(): pl.pallas_call(main_kernel, out_shape=jax.ShapeDtypeStruct((GRP // NZ, NZ...  124 us
    unnamed x9, local copies, waits for them, and re-layouts  4.19 us

profile of v1, /device:TPU:1, one launch (start us, length us, event | category | flops | bytes accessed | tf_op | source)
XLA Modules:
  0.0 130.0 jit_solution(18988221279856539)
XLA Ops:
  0.0 2.1 %shard_map.64.table = s32[96]{0:T(128)} custom-call(s32[48]{0:T(128)} %bitcast.10, s32[48]{0:T(128)} %bitcast.11), custom_call_target="tpu_custom_call" | custom-call | tf_op jit(solution)/shard_map/pallas_call | solution.py:346
  2.1 0.0 copy-start
  2.1 1.0 copy-done
  3.2 0.0 copy-start.1
  3.2 0.9 copy-done.1
  4.1 0.0 copy-start.2
  4.1 0.8 copy-done.2
  5.0 0.0 copy-start.3
  5.0 0.7 copy-done.3
  5.6 123.7 %shard_map.65 = bf16[4,8,16,256]{3,2,1,0:T(8,128)(2,1)S(1)} custom-call(s32[96]{0:T(128)S(1)} %copy-done.3, bf16[128,1024]{1,0:T(8,128)(2,1)S(1)} %bitcast.7, bf16[128,256]{1,0:T(8,128)(2,1)S(1)} %bitcast.8, bf16[48,128,256]{2,1,0:T(8,128)(2,1)} %bitcast.9, bf16[1024,256]{1,0:T(8,128)(2,1)S(1)} %copy-done), custom_call_target="tpu_custom_call" | custom-call | tf_op jit(solution)/shard_map/pallas_call | solution.py:354
  129.3 0.7 copy.8
Async XLA Ops:
  2.1 1.0 copy-start
  3.2 0.9 copy-start.1
  4.1 0.8 copy-start.2
  5.0 0.7 copy-start.3

commit v2 on v1

v2 whole, which is shorter than its diff:
```python
import functools

import jax
import jax.numpy as jnp
from jax import lax
from jax.experimental import pallas as pl
from jax.experimental.pallas import tpu as pltpu
from jax.sharding import PartitionSpec as P

MESH = pl.DeviceIdType.MESH
NX, NY, NC, NZ = 4, 4, 2, 8
GRP = NX * NY * NC
CAP = 2
KB = 128
HD = 128
NEW = 128
WIDTH = 1024
FEAT = 256
CHUNK = NEW // NZ
NEG = -1e30
AHEAD = 31
STOPS = (1, 9, 17)
VMEM_LIMIT = 62 * 1024 * 1024
LOG2E = 1.4426950408889634
F32 = jnp.float32
BF16 = jnp.bfloat16
ORDER = ((0, 0), (3, 0), (1, 0), (0, 3), (0, 1), (2, 0), (3, 3), (3, 1), (1, 3), (1, 1), (0, 2), (2, 3), (2, 1), (3, 2), (1, 2), (2, 2))


def main_kernel(
    owner_hbm, fill_hbm, q_hbm, span_hbm, cache_hbm, w_hbm, o_ref,
    owner_ref, fill_ref, q_ref, span_ref, cache_ref, table_v, table,
    send, sfill, recv, rfill, qs, m, acc, wfull, heads, gath, total, zout, obuf,
    in_s, kv_s, kv_r, f_s, f_r, w_s, w_r, a_s, a_r, g_s, g_r, b_s, b_r, o_s, o_r,
):
    g = lax.axis_index("grp")
    t = lax.axis_index("tp")
    x, y, c = g // (NY * NC), (g // NC) % NY, g % NC

    def at(px, py, pc):
        return (px % NX) * (NY * NC) + (py % NY) * NC + pc

    sib = at(x, y, 1 - c)

    def copy(src, dst, ssem, rsem, dev):
        return pltpu.make_async_remote_copy(
            src_ref=src, dst_ref=dst, send_sem=ssem, recv_sem=rsem, device_id=dev, device_id_type=MESH
        )

    barrier = pltpu.get_barrier_semaphore()

    def greet(s, k):
        pl.semaphore_signal(barrier, inc=1, device_id=((g + s) % GRP, t), device_id_type=MESH)
        return k

    lax.fori_loop(1, GRP, greet, 0)
    for s in range(1, NZ):
        pl.semaphore_signal(barrier, inc=1, device_id=(g, (t + s) % NZ), device_id_type=MESH)
    loads = [
        pltpu.make_async_copy(owner_hbm, owner_ref, in_s.at[0]),
        pltpu.make_async_copy(fill_hbm, fill_ref, in_s.at[1]),
        pltpu.make_async_copy(cache_hbm, cache_ref, in_s.at[2]),
        pltpu.make_async_copy(w_hbm, wfull.at[t], in_s.at[3]),
        pltpu.make_async_copy(q_hbm, q_ref, in_s.at[4]),
        pltpu.make_async_copy(span_hbm, span_ref, in_s.at[5]),
    ]
    for d in loads:
        d.start()

    loads[0].wait()
    loads[1].wait()
    slots = owner_ref.shape[1]
    shape = (GRP, slots)
    own = jnp.broadcast_to(owner_ref[...], shape)
    fill = jnp.broadcast_to(fill_ref[...], shape)
    block = lax.broadcasted_iota(jnp.int32, shape, 1)
    hit = own == lax.broadcasted_iota(jnp.int32, shape, 0)
    low = jnp.min(jnp.where(hit, block, slots), 1, keepdims=True)
    high = jnp.max(jnp.where(hit, block, -1), 1, keepdims=True)
    code = jnp.sum(jnp.where(hit, jnp.where(block == low, fill, fill * 256), 0), 1, keepdims=True)
    lane = lax.broadcasted_iota(jnp.int32, (GRP, KB), 1)
    table_v[...] = jnp.where(lane == 0, jnp.minimum(low, slots - 1), jnp.maximum(high, 0))
    sfill[...] = jnp.broadcast_to(code, (GRP, KB)).reshape(GRP, 1, KB)
    to_smem = pltpu.make_async_copy(table_v, table, in_s.at[6])
    to_smem.start()
    to_smem.wait()
    loads[2].wait()

    def load(dst):
        return cache_ref[table[dst, 0]], cache_ref[table[dst, 1]]

    def pack(s, k):
        dst = (g + s) % GRP
        first, second = load(dst)
        send[dst, :KB] = first
        send[dst, KB:] = second
        return k

    lax.fori_loop(1, GRP, pack, 0)
    first, second = load(g)
    recv[g, :KB] = first
    recv[g, KB:] = second
    rfill[g] = sfill[g]
    loads[3].wait()
    pl.semaphore_wait(barrier, GRP - 1 + NZ - 1)

    up, down = (t + 1) % NZ, (t + NZ - 1) % NZ
    half = WIDTH // 2

    def wcopy(n, z, lo, size, k, dev):
        part = wfull.at[z, pl.ds(lo, size)]
        return copy(part, part, w_s.at[n], w_r.at[z, k], (g, dev))

    wsends = [wcopy(0, t, 0, WIDTH, 0, up), wcopy(1, t, 0, WIDTH, 0, down)]
    for d in wsends:
        d.start()

    def wpass(j, lo, hi):
        low, high = (t + NZ - j) % NZ, (t + j) % NZ
        wcopy(0, low, 0, WIDTH, 0, up).wait_recv()
        d0 = wcopy(2 * j, low, lo, hi, 0, up)
        d0.start()
        wcopy(0, high, 0, WIDTH, 0, down).wait_recv()
        d1 = wcopy(2 * j + 1, high, half if hi < WIDTH else 0, hi, 1 if hi < WIDTH else 0, down)
        d1.start()
        wsends.extend([d0, d1])

    def where_to(s):
        o = (s * 11) % GRP
        return o // (NY * NC), (o // NC) % NY, o % NC

    def kv_copy(dst, s):
        return copy(send.at[dst], recv.at[g], kv_s.at[s], kv_r.at[g], (dst, t))

    def fill_copy(dst, s):
        return copy(sfill.at[dst], rfill.at[g], f_s.at[s], f_r.at[g], (dst, t))

    def give(s, k):
        dx, dy, dc = where_to(s)
        dst = at(x + dx, y + dy, (c + dc) % NC)
        kv_copy(dst, s).start()
        fill_copy(dst, s).start()
        return k

    lax.fori_loop(1, AHEAD + 1, give, 0)
    loads[4].wait()
    loads[5].wait()

    heads_n = WIDTH // HD
    for h in range(heads_n):
        qs[h * NEW:(h + 1) * NEW, :] = q_ref[:, h * HD:(h + 1) * HD]
    factor = LOG2E / HD**0.5
    blk = 256
    ones = jnp.ones((CAP * KB, HD), BF16)

    def scores(rows, keys):
        return lax.dot_general(qs[rows, :], keys, (((1,), (1,)), ((), ())), preferred_element_type=F32) * factor

    span_k, span_v = span_ref[:, :HD], span_ref[:, HD:]
    span_aug = jnp.concatenate([span_v, ones[:NEW]], 1)
    row = lax.broadcasted_iota(jnp.int32, (blk, NEW), 0) % NEW
    col = lax.broadcasted_iota(jnp.int32, (blk, NEW), 1)
    for qb in range(WIDTH // blk):
        rows = pl.ds(qb * blk, blk)
        s = jnp.where(col <= row, scores(rows, span_k), NEG)
        top = jnp.max(s, 1, keepdims=True)
        m[rows, :] = jnp.broadcast_to(top, (blk, HD))
        p = jnp.exp2(s - top).astype(BF16)
        acc[rows, :] = jnp.dot(p, span_aug, preferred_element_type=F32)

    lane = lax.broadcasted_iota(jnp.int32, (1, KB), 1)

    def attend(src):
        fills = rfill[src]
        bias = jnp.concatenate(
            [jnp.where(lane < fills % 256, 0.0, NEG), jnp.where(lane < fills // 256, 0.0, NEG)], 1
        )
        keys = recv[src, :, :HD]
        vals = jnp.concatenate([recv[src, :, HD:], ones], 1)
        for qb in range(WIDTH // blk):
            rows = pl.ds(qb * blk, blk)
            s = scores(rows, keys) + bias
            old = m[rows, :]
            new = jnp.maximum(old, jnp.max(s, 1, keepdims=True))
            alpha = jnp.exp2(old - new)
            p = jnp.exp2(s - jnp.concatenate([new, new], 1)).astype(BF16)
            part = jnp.dot(p, vals, preferred_element_type=F32)
            acc[rows, :] = acc[rows, :] * jnp.concatenate([alpha, alpha], 1) + part
            m[rows, :] = new

    attend(g)

    def take(s, k):
        dx, dy, dc = where_to(s)
        src = at(x + NX - dx, y + NY - dy, (c + dc) % NC)
        copy(send.at[src], recv.at[src], kv_s.at[s], kv_r.at[src], (src, t)).wait_recv()
        copy(sfill.at[src], rfill.at[src], f_s.at[s], f_r.at[src], (src, t)).wait_recv()
        attend(src)
        return k

    def take_give(s, k):
        give(s + AHEAD, k)
        return take(s, k)

    def run(lo, hi):
        split = min(max(GRP - AHEAD, lo), hi)
        if lo < split:
            lax.fori_loop(lo, split, take_give, 0)
        if split < hi:
            lax.fori_loop(split, hi, take, 0)

    run(1, STOPS[0])
    wpass(1, 0, WIDTH)
    run(STOPS[0], STOPS[1])
    wpass(2, 0, WIDTH)
    run(STOPS[1], STOPS[2])
    wpass(3, 0, half)
    total[...] = jnp.zeros_like(total)
    run(STOPS[2], GRP)

    per_half = heads_n // 2

    def zcopy(hf, s, dst):
        z = (t + s) % NZ
        return copy(heads.at[hf, z], gath.at[g, hf, dst(z)], a_s.at[hf, s], a_r.at[hf, dst(z)], (g, z))

    for hf in range(2):
        for h in range(per_half):
            rows = pl.ds((hf * per_half + h) * NEW, NEW)
            out = (acc[rows, :HD] / acc[rows, HD:]).astype(BF16)
            heads[hf, :, :, h * HD:(h + 1) * HD] = out.reshape(NZ, CHUNK, HD)
        for s in range(1, NZ):
            zcopy(hf, s, lambda z: t).start()
        gath[g, hf, t] = heads[hf, t]

    def spread_in(hf):
        for s in range(1, NZ):
            zcopy(hf, s, lambda z: z).wait_recv()

    sends = []

    def piece(owner, lo, size):
        return gath.at[owner, lo // NZ, pl.ds(lo % NZ, size)]

    def push(owner, lo, size, quarter, dev):
        part = piece(owner, lo, size)
        d = copy(part, part, g_s.at[len(sends)], g_r.at[owner, quarter], (dev, t))
        d.start()
        sends.append(d)

    def arrived(owner, lo, size, quarter):
        part = piece(owner, lo, size)
        copy(part, part, g_s.at[0], g_r.at[owner, quarter], (sib, t)).wait_recv()

    def place(h, d1, d2, pc):
        return at(x + d1, y + d2, pc) if h == 0 else at(x + d2, y + d1, pc)

    def share(h, owner):
        part = piece(owner, NZ * h, NZ)
        d = copy(part, part, b_s.at[len(shared)], b_r.at[owner, h], (sib, t))
        d.start()
        shared.append(d)

    shared = []

    def event(h, d1, d2):
        owner = place(h, d1, d2, c)
        lo = NZ * h
        q = 2 * h
        fwd1, back1 = place(h, 1, 0, c), place(h, 3, 0, c)
        fwd2, back2 = place(h, 0, 1, c), place(h, 0, 3, c)
        last = d2 if d2 else d1
        if last == 2:
            arrived(owner, lo, 4, q)
            arrived(owner, lo + 4, 4, q + 1)
        elif last:
            arrived(owner, lo, NZ, q)
        if d2 == 0:
            if d1 == 0:
                push(owner, lo, NZ, q, fwd1)
                push(owner, lo, NZ, q, back1)
            elif d1 == 3:
                push(owner, lo, 4, q, fwd1)
            elif d1 == 1:
                push(owner, lo + 4, 4, q + 1, back1)
            push(owner, lo, NZ, q, fwd2)
            push(owner, lo, NZ, q, back2)
        elif d2 == 3:
            push(owner, lo, 4, q, fwd2)
        elif d2 == 1:
            push(owner, lo + 4, 4, q + 1, back2)
        share(h, owner)

    def multiply(h, d2):
        owners = [place(h, d1, d2, pc) for d1 in range(4) for pc in range(2)]
        for d1 in range(4):
            other = place(h, d1, d2, 1 - c)
            part = piece(other, NZ * h, NZ)
            copy(part, part, b_s.at[0], b_r.at[other, h], (sib, t)).wait_recv()

        def step(z, sum_):
            rows = jnp.concatenate([gath[o, h, z] for o in owners], 0)
            return sum_ + jnp.dot(rows, wfull[z, h * half:(h + 1) * half], preferred_element_type=F32)

        got = lax.fori_loop(0, NZ, step, jnp.zeros((len(owners) * CHUNK, FEAT), F32))
        for i, o in enumerate(owners):
            total[o] = total[o] + got[i * CHUNK:(i + 1) * CHUNK]

    def ocopy(s, e, dst):
        z = (t + s) % NZ
        to = dst(z)
        here = z * 4 + e * 2 if to is t else t * 4 + e * 2
        return copy(
            zout.at[pl.ds(here, 2)], obuf.at[pl.ds(e * 2, 2), to], o_s.at[s, e], o_r.at[to, e], (g, z)
        )

    def hand(late):
        for s in range(1, NZ):
            z = (t + s) % NZ
            for e in range(2):
                far = ((z // 2 + NX - x) % NX == 2) | (((z % 2) * 2 + e + NY - y) % NY == 2)

                @pl.when(far if late else jnp.logical_not(far))
                def _():
                    ocopy(s, e, lambda z: t).start()

    for n, (d1, d2) in enumerate(ORDER):
        for h in range(2):
            if n == 0:
                spread_in(h)
            event(h, d1, d2)
        if n == 5:
            opposite = (t + 4) % NZ
            wcopy(0, opposite, 0, half, 0, up).wait_recv()
            wcopy(0, opposite, half, half, 1, down).wait_recv()
        if n in (6, 7):
            multiply(n - 6, 0)
        if n == 12:
            for h in range(2):
                multiply(h, 3)
                multiply(h, 1)
            zout[...] = total[...].astype(BF16)
            hand(False)
    for h in range(2):
        multiply(h, 2)

    def finish(o):
        zout[o] = total[o].astype(BF16)

    for i in range(NX):
        for pc in range(NC):
            finish(at(x + 2, i, pc))
            if i:
                finish(at(x + 2 + i, y + 2, pc))
    hand(True)
    obuf[:, t] = zout[pl.ds(t * 4, 4)]
    for s in range(1, NZ):
        for e in range(2):
            ocopy(s, e, lambda z: z).wait_recv()
    o_ref[...] = obuf[...]

    def sent(s, k):
        dx, dy, dc = where_to(s)
        dst = at(x + dx, y + dy, (c + dc) % NC)
        kv_copy(dst, s).wait_send()
        fill_copy(dst, s).wait_send()
        return k

    lax.fori_loop(1, GRP, sent, 0)

    for s in range(1, NZ):
        for e in range(2):
            zcopy(e, s, lambda z: t).wait_send()
            ocopy(s, e, lambda z: t).wait_send()
    for d in wsends + sends + shared:
        d.wait_send()


def body(queries, span_kv, cache, block_owner, block_fill, out_weight):
    slots = cache.shape[0]
    any_ = pl.BlockSpec(memory_space=pl.ANY)
    vmem = pl.BlockSpec(memory_space=pltpu.VMEM)
    dma = pltpu.SemaphoreType.DMA
    out = pl.pallas_call(
        main_kernel,
        out_shape=jax.ShapeDtypeStruct((GRP // NZ, NZ, CHUNK, FEAT), BF16),
        in_specs=[any_] * 6,
        out_specs=vmem,
        scratch_shapes=[
            pltpu.VMEM((1, slots), jnp.int32),
            pltpu.VMEM((1, slots), jnp.int32),
            pltpu.VMEM((NEW, WIDTH), BF16),
            pltpu.VMEM((NEW, 2 * HD), BF16),
            pltpu.VMEM((slots, KB, 2 * HD), BF16),
            pltpu.VMEM((GRP, KB), jnp.int32),
            pltpu.SMEM((GRP, KB), jnp.int32),
            pltpu.VMEM((GRP, CAP * KB, 2 * HD), BF16),
            pltpu.VMEM((GRP, 1, KB), jnp.int32),
            pltpu.VMEM((GRP, CAP * KB, 2 * HD), BF16),
            pltpu.VMEM((GRP, 1, KB), jnp.int32),
            pltpu.VMEM((WIDTH, HD), BF16),
            pltpu.VMEM((WIDTH, HD), F32),
            pltpu.VMEM((WIDTH, 2 * HD), F32),
            pltpu.VMEM((NZ, WIDTH, FEAT), BF16),
            pltpu.VMEM((2, NZ, CHUNK, WIDTH // 2), BF16),
            pltpu.VMEM((GRP, 2, NZ, CHUNK, WIDTH // 2), BF16),
            pltpu.VMEM((GRP, CHUNK, FEAT), F32),
            pltpu.VMEM((GRP, CHUNK, FEAT), BF16),
            pltpu.VMEM((GRP // NZ, NZ, CHUNK, FEAT), BF16),
            dma((7,)),
            dma((GRP,)), dma((GRP,)), dma((GRP,)), dma((GRP,)),
            dma((NZ,)), dma((NZ, 2)),
            dma((2, NZ)), dma((2, NZ)),
            dma((40,)), dma((GRP, 4)),
            dma((32,)), dma((GRP, 2)),
            dma((NZ, 2)), dma((NZ, 2)),
        ],
        compiler_params=pltpu.CompilerParams(
            collective_id=0, has_side_effects=True, vmem_limit_bytes=VMEM_LIMIT
        ),
    )(
        block_owner.reshape(1, slots),
        block_fill.reshape(1, slots),
        queries.reshape(NEW, WIDTH),
        span_kv.reshape(NEW, 2 * HD),
        cache.reshape(slots, KB, 2 * HD),
        out_weight,
    )
    return out.reshape(GRP // NZ * NEW, FEAT)


def solution(mesh):
    in_specs = (
        P("grp", None, "tp"),
        P("grp", None, "tp", None),
        P("grp", None, "tp", None),
        P("grp", None),
        P("grp", None),
        P("tp", "grp"),
    )
    out_specs = P("tp", "grp")
    return jax.shard_map(body, mesh=mesh, in_specs=in_specs, out_specs=out_specs, check_vma=False)
```

time: 130 us -> 114 us (0.88)
  the two profiles are of different devices: /device:TPU:1 before, /device:TPU:5 now
where the time goes in v2:
time: 114 us
  Pallas kernels  112 us (98%)
  local copies, waits for them, and re-layouts  1.67 us (1%)
    pallas_call x1, Pallas kernels, body(): pl.pallas_call(main_kernel, out_shape=jax.ShapeDtypeStruct((GRP // NZ, NZ...  112 us

profile of v2, /device:TPU:5, one launch (start us, length us, event | category | flops | bytes accessed | tf_op | source)
XLA Modules:
  0.0 114.1 jit_solution(3052952389141094817)
XLA Ops:
  0.0 112.4 %shard_map.64 = bf16[4,8,16,256]{3,2,1,0:T(8,128)(2,1)} custom-call(s32[1,48]{1,0:T(1,128)} %bitcast.10, s32[1,48]{1,0:T(1,128)} %bitcast.11, bf16[128,1024]{1,0:T(8,128)(2,1)} %bitcast.8, bf16[128,256]{1,0:T(8,128)(2,1)} %bitcast.9, bf16[48,128,256]{2,1,0:T(8,128)(2,1)} %bitcast.6, bf16[1024,256]{1,0:T(8,128)(2,1)} %w_hbm.1), custom_call_target="tpu_custom_call" | custom-call | tf_op jit(solution)/shard_map/pallas_call | solution.py:384
  112.4 1.7 %copy.8 = bf16[512,256]{1,0:T(8,128)(2,1)} copy(bf16[512,256]{1,0:T(8,128)(2,1)} %bitcast.7) | data formatting | bytes 524288

commit v3 on v2

--- a/solution.py
+++ b/solution.py
@@ -9,7 +9,8 @@
 
 MESH = pl.DeviceIdType.MESH
 NX, NY, NC, NZ = 4, 4, 2, 8
-GRP = NX * NY * NC
+CHIPS = NX * NY
+GRP = CHIPS * NC
 CAP = 2
 KB = 128
 HD = 128
@@ -18,8 +19,8 @@
 FEAT = 256
 CHUNK = NEW // NZ
 NEG = -1e30
-AHEAD = 31
-STOPS = (1, 9, 17)
+EARLY = 12
+SWITCH = 20
 VMEM_LIMIT = 62 * 1024 * 1024
 LOG2E = 1.4426950408889634
 F32 = jnp.float32
@@ -111,38 +112,61 @@
         part = wfull.at[z, pl.ds(lo, size)]
         return copy(part, part, w_s.at[n], w_r.at[z, k], (g, dev))
 
-    wsends = [wcopy(0, t, 0, WIDTH, 0, up), wcopy(1, t, 0, WIDTH, 0, down)]
-    for d in wsends:
+    WSENDS = [
+        (0, 0, 0, WIDTH, 0, 1), (1, 0, 0, WIDTH, 0, -1), (2, -1, 0, WIDTH, 0, 1), (3, 1, 0, WIDTH, 0, -1),
+        (4, -2, 0, WIDTH, 0, 1), (5, 2, 0, WIDTH, 0, -1), (6, -3, 0, half, 0, 1), (7, 3, half, half, 1, -1),
+    ]
+
+    def wsend(n):
+        n, dz, lo, size, k, way = WSENDS[n]
+        return wcopy(n, (t + NZ + dz) % NZ, lo, size, k, up if way == 1 else down)
+
+    wsend(0).start()
+    wsend(1).start()
+
+    def wpass(j):
+        wcopy(0, (t + NZ - j) % NZ, 0, WIDTH, 0, up).wait_recv()
+        wsend(2 * j).start()
+        wcopy(0, (t + j) % NZ, 0, WIDTH, 0, down).wait_recv()
+        wsend(2 * j + 1).start()
+
+    def wlast():
+        opposite = (t + 4) % NZ
+        wcopy(0, opposite, 0, half, 0, up).wait_recv()
+        wcopy(0, opposite, half, half, 1, down).wait_recv()
+
+    def hop(k):
+        o = (k * 5) % CHIPS
+        return o // NY, o % NY
+
+    def kv_copies(dst, n):
+        return (
+            copy(send.at[dst], recv.at[g], kv_s.at[n], kv_r.at[g], (dst, t)),
+            copy(sfill.at[dst], rfill.at[g], f_s.at[n], f_r.at[g], (dst, t)),
+        )
+
+    def give_to(p, k):
+        dx, dy = hop(k)
+        return kv_copies(at(x + dx, y + dy, p), p * CHIPS + k)
+
+    def give(p, k, carry):
+        for d in give_to(p, k):
+            d.start()
+        return carry
+
+    for d in kv_copies(sib, 0):
         d.start()
-
-    def wpass(j, lo, hi):
-        low, high = (t + NZ - j) % NZ, (t + j) % NZ
-        wcopy(0, low, 0, WIDTH, 0, up).wait_recv()
-        d0 = wcopy(2 * j, low, lo, hi, 0, up)
-        d0.start()
-        wcopy(0, high, 0, WIDTH, 0, down).wait_recv()
-        d1 = wcopy(2 * j + 1, high, half if hi < WIDTH else 0, hi, 1 if hi < WIDTH else 0, down)
-        d1.start()
-        wsends.extend([d0, d1])
-
-    def where_to(s):
-        o = (s * 11) % GRP
-        return o // (NY * NC), (o // NC) % NY, o % NC
-
-    def kv_copy(dst, s):
-        return copy(send.at[dst], recv.at[g], kv_s.at[s], kv_r.at[g], (dst, t))
-
-    def fill_copy(dst, s):
-        return copy(sfill.at[dst], rfill.at[g], f_s.at[s], f_r.at[g], (dst, t))
-
-    def give(s, k):
-        dx, dy, dc = where_to(s)
-        dst = at(x + dx, y + dy, (c + dc) % NC)
-        kv_copy(dst, s).start()
-        fill_copy(dst, s).start()
-        return k
-
-    lax.fori_loop(1, AHEAD + 1, give, 0)
+    lax.fori_loop(1, CHIPS, functools.partial(give, 0), 0)
+
+    def more():
+        def done(k, carry):
+            for d in give_to(0, k):
+                d.wait_send()
+            return carry
+
+        lax.fori_loop(1, EARLY + 1, done, 0)
+        lax.fori_loop(1, CHIPS, functools.partial(give, 1), 0)
+
     loads[4].wait()
     loads[5].wait()
 
@@ -188,35 +212,25 @@
             acc[rows, :] = acc[rows, :] * jnp.concatenate([alpha, alpha], 1) + part
             m[rows, :] = new
 
+    def take_from(src):
+        for d in (
+            copy(send.at[src], recv.at[src], kv_s.at[0], kv_r.at[src], (src, t)),
+            copy(sfill.at[src], rfill.at[src], f_s.at[0], f_r.at[src], (src, t)),
+        ):
+            d.wait_recv()
+        attend(src)
+
+    def take(i, k):
+        dx, dy = hop(i // NC)
+        take_from(at(x + NX - dx, y + NY - dy, i % NC))
+        return k
+
+    def run(lo, hi):
+        lax.fori_loop(lo, hi, take, 0)
+
     attend(g)
-
-    def take(s, k):
-        dx, dy, dc = where_to(s)
-        src = at(x + NX - dx, y + NY - dy, (c + dc) % NC)
-        copy(send.at[src], recv.at[src], kv_s.at[s], kv_r.at[src], (src, t)).wait_recv()
-        copy(sfill.at[src], rfill.at[src], f_s.at[s], f_r.at[src], (src, t)).wait_recv()
-        attend(src)
-        return k
-
-    def take_give(s, k):
-        give(s + AHEAD, k)
-        return take(s, k)
-
-    def run(lo, hi):
-        split = min(max(GRP - AHEAD, lo), hi)
-        if lo < split:
-            lax.fori_loop(lo, split, take_give, 0)
-        if split < hi:
-            lax.fori_loop(split, hi, take, 0)
-
-    run(1, STOPS[0])
-    wpass(1, 0, WIDTH)
-    run(STOPS[0], STOPS[1])
-    wpass(2, 0, WIDTH)
-    run(STOPS[1], STOPS[2])
-    wpass(3, 0, half)
+    take_from(sib)
     total[...] = jnp.zeros_like(total)
-    run(STOPS[2], GRP)
 
     per_half = heads_n // 2
 
@@ -224,29 +238,26 @@
         z = (t + s) % NZ
         return copy(heads.at[hf, z], gath.at[g, hf, dst(z)], a_s.at[hf, s], a_r.at[hf, dst(z)], (g, z))
 
-    for hf in range(2):
-        for h in range(per_half):
-            rows = pl.ds((hf * per_half + h) * NEW, NEW)
-            out = (acc[rows, :HD] / acc[rows, HD:]).astype(BF16)
-            heads[hf, :, :, h * HD:(h + 1) * HD] = out.reshape(NZ, CHUNK, HD)
+    def spread(hf):
         for s in range(1, NZ):
             zcopy(hf, s, lambda z: t).start()
         gath[g, hf, t] = heads[hf, t]
 
+    def finalize():
+        for hf in range(2):
+            for h in range(per_half):
+                rows = pl.ds((hf * per_half + h) * NEW, NEW)
+                out = (acc[rows, :HD] / acc[rows, HD:]).astype(BF16)
+                heads[hf, :, :, h * HD:(h + 1) * HD] = out.reshape(NZ, CHUNK, HD)
+            if hf == 0:
+                spread(0)
+
     def spread_in(hf):
         for s in range(1, NZ):
             zcopy(hf, s, lambda z: z).wait_recv()
 
-    sends = []
-
     def piece(owner, lo, size):
         return gath.at[owner, lo // NZ, pl.ds(lo % NZ, size)]
-
-    def push(owner, lo, size, quarter, dev):
-        part = piece(owner, lo, size)
-        d = copy(part, part, g_s.at[len(sends)], g_r.at[owner, quarter], (dev, t))
-        d.start()
-        sends.append(d)
 
     def arrived(owner, lo, size, quarter):
         part = piece(owner, lo, size)
@@ -255,125 +266,191 @@
     def place(h, d1, d2, pc):
         return at(x + d1, y + d2, pc) if h == 0 else at(x + d2, y + d1, pc)
 
-    def share(h, owner):
+    PUSHES = {
+        (0, 0): [((1, 0), 0, NZ, 0), ((3, 0), 0, NZ, 0), ((0, 1), 0, NZ, 0), ((0, 3), 0, NZ, 0)],
+        (3, 0): [((1, 0), 0, 4, 0), ((0, 1), 0, NZ, 0), ((0, 3), 0, NZ, 0)],
+        (1, 0): [((3, 0), 4, 4, 1), ((0, 1), 0, NZ, 0), ((0, 3), 0, NZ, 0)],
+        (2, 0): [((0, 1), 0, NZ, 0), ((0, 3), 0, NZ, 0)],
+    }
+    for d1 in range(4):
+        PUSHES[(d1, 3)] = [((0, 1), 0, 4, 0)]
+        PUSHES[(d1, 1)] = [((0, 3), 4, 4, 1)]
+    first_sem, count = {}, 0
+    for h in range(2):
+        for d in ORDER:
+            first_sem[(h, d)] = count
+            count += len(PUSHES.get(d, ()))
+
+    def pushes(h, d1, d2):
+        owner = place(h, d1, d2, c)
+        base = first_sem[(h, (d1, d2))]
+        out = []
+        for i, (to, lo, size, quarter) in enumerate(PUSHES.get((d1, d2), ())):
+            part = piece(owner, NZ * h + lo, size)
+            dev = place(h, to[0], to[1], c)
+            out.append(copy(part, part, g_s.at[base + i], g_r.at[owner, 2 * h + quarter], (dev, t)))
+        return out
+
+    def share(h, d1, d2):
+        owner = place(h, d1, d2, c)
         part = piece(owner, NZ * h, NZ)
-        d = copy(part, part, b_s.at[len(shared)], b_r.at[owner, h], (sib, t))
-        d.start()
-        shared.append(d)
-
-    shared = []
+        n = h * CHIPS + ORDER.index((d1, d2))
+        return copy(part, part, b_s.at[n], b_r.at[owner, h], (sib, t))
 
     def event(h, d1, d2):
         owner = place(h, d1, d2, c)
         lo = NZ * h
         q = 2 * h
-        fwd1, back1 = place(h, 1, 0, c), place(h, 3, 0, c)
-        fwd2, back2 = place(h, 0, 1, c), place(h, 0, 3, c)
         last = d2 if d2 else d1
         if last == 2:
             arrived(owner, lo, 4, q)
             arrived(owner, lo + 4, 4, q + 1)
         elif last:
             arrived(owner, lo, NZ, q)
-        if d2 == 0:
-            if d1 == 0:
-                push(owner, lo, NZ, q, fwd1)
-                push(owner, lo, NZ, q, back1)
-            elif d1 == 3:
-                push(owner, lo, 4, q, fwd1)
-            elif d1 == 1:
-                push(owner, lo + 4, 4, q + 1, back1)
-            push(owner, lo, NZ, q, fwd2)
-            push(owner, lo, NZ, q, back2)
-        elif d2 == 3:
-            push(owner, lo, 4, q, fwd2)
-        elif d2 == 1:
-            push(owner, lo + 4, 4, q + 1, back2)
-        share(h, owner)
-
-    def multiply(h, d2):
-        owners = [place(h, d1, d2, pc) for d1 in range(4) for pc in range(2)]
-        for d1 in range(4):
-            other = place(h, d1, d2, 1 - c)
-            part = piece(other, NZ * h, NZ)
-            copy(part, part, b_s.at[0], b_r.at[other, h], (sib, t)).wait_recv()
-
-        def step(z, sum_):
-            rows = jnp.concatenate([gath[o, h, z] for o in owners], 0)
-            return sum_ + jnp.dot(rows, wfull[z, h * half:(h + 1) * half], preferred_element_type=F32)
-
-        got = lax.fori_loop(0, NZ, step, jnp.zeros((len(owners) * CHUNK, FEAT), F32))
+        for d in pushes(h, d1, d2):
+            d.start()
+        share(h, d1, d2).start()
+
+    def shared_in(h, groups):
+        for d2 in groups:
+            for d1 in range(4):
+                other = place(h, d1, d2, 1 - c)
+                part = piece(other, NZ * h, NZ)
+                copy(part, part, b_s.at[0], b_r.at[other, h], (sib, t)).wait_recv()
+
+    def multiply(h, groups, *pcs):
+        owners = [place(h, d1, d2, pc) for pc in pcs for d2 in groups for d1 in range(4)]
+        rows = jnp.concatenate(
+            [jnp.concatenate([gath[o, h, z] for o in owners], 0) for z in range(NZ)], 1
+        )
+        weights = wfull[:, h * half:(h + 1) * half].reshape(NZ * half, FEAT)
+        got = jnp.dot(rows, weights, preferred_element_type=F32)
         for i, o in enumerate(owners):
             total[o] = total[o] + got[i * CHUNK:(i + 1) * CHUNK]
 
-    def ocopy(s, e, dst):
+    def ocopy(s, e, pc, dst):
         z = (t + s) % NZ
         to = dst(z)
-        here = z * 4 + e * 2 if to is t else t * 4 + e * 2
-        return copy(
-            zout.at[pl.ds(here, 2)], obuf.at[pl.ds(e * 2, 2), to], o_s.at[s, e], o_r.at[to, e], (g, z)
-        )
-
-    def hand(late):
+        here = z * 4 + e * 2 + pc if to is t else t * 4 + e * 2 + pc
+        return copy(zout.at[here], obuf.at[e * 2 + pc, to], o_s.at[s, e, pc], o_r.at[to, e, pc], (g, z))
+
+    def hand(pc, late):
         for s in range(1, NZ):
             z = (t + s) % NZ
             for e in range(2):
+                if late is None:
+                    ocopy(s, e, pc, lambda z: t).start()
+                    continue
                 far = ((z // 2 + NX - x) % NX == 2) | (((z % 2) * 2 + e + NY - y) % NY == 2)
 
                 @pl.when(far if late else jnp.logical_not(far))
                 def _():
-                    ocopy(s, e, lambda z: t).start()
-
-    for n, (d1, d2) in enumerate(ORDER):
+                    ocopy(s, e, pc, lambda z: t).start()
+
+    def finish(pc, late):
+        for d1 in range(4):
+            for d2 in range(4):
+                if late is None or late == (d1 == 2 or d2 == 2):
+                    o = at(x + d1, y + d2, pc)
+                    zout[o] = total[o].astype(BF16)
+        hand(pc, late)
+
+    near = (0, 3, 1)
+    every = (0, 3, 1, 2)
+
+    def events(lo, hi):
+        for d in ORDER[lo:hi]:
+            for h in range(2):
+                event(h, *d)
+
+    def opening():
+        finalize()
+        spread(1)
+        spread_in(0)
+        event(0, 0, 0)
+        spread_in(1)
+        event(1, 0, 0)
+
+    @pl.when(c == 0)
+    def _():
+        wpass(1)
+        run(2, 12)
+        wpass(2)
+        run(12, 20)
+        more()
+        run(20, GRP)
+        opening()
+        events(1, 5)
+        wpass(3)
+        events(5, 16)
+        wlast()
         for h in range(2):
-            if n == 0:
-                spread_in(h)
-            event(h, d1, d2)
-        if n == 5:
-            opposite = (t + 4) % NZ
-            wcopy(0, opposite, 0, half, 0, up).wait_recv()
-            wcopy(0, opposite, half, half, 1, down).wait_recv()
-        if n in (6, 7):
-            multiply(n - 6, 0)
-        if n == 12:
-            for h in range(2):
-                multiply(h, 3)
-                multiply(h, 1)
-            zout[...] = total[...].astype(BF16)
-            hand(False)
-    for h in range(2):
-        multiply(h, 2)
-
-    def finish(o):
-        zout[o] = total[o].astype(BF16)
-
-    for i in range(NX):
-        for pc in range(NC):
-            finish(at(x + 2, i, pc))
-            if i:
-                finish(at(x + 2 + i, y + 2, pc))
-    hand(True)
+            multiply(h, every, 0)
+        finish(0, None)
+        for h in range(2):
+            shared_in(h, near)
+            multiply(h, near, 1)
+        finish(1, False)
+        for h in range(2):
+            shared_in(h, (2,))
+            multiply(h, (2,), 1)
+
+    @pl.when(c == 1)
+    def _():
+        wpass(1)
+        wpass(2)
+        more()
+        run(2, 10)
+        wpass(3)
+        run(10, GRP)
+        opening()
+        events(1, 4)
+        wlast()
+        shared_in(0, every)
+        multiply(0, every, 0)
+        events(4, 8)
+        shared_in(1, every)
+        multiply(1, every, 0)
+        events(8, 13)
+        finish(0, None)
+        multiply(0, near, 1)
+        events(13, 14)
+        multiply(1, near, 1)
+        events(14, 16)
+        finish(1, False)
+        for h in range(2):
+            multiply(h, (2,), 1)
+
+    finish(1, True)
     obuf[:, t] = zout[pl.ds(t * 4, 4)]
     for s in range(1, NZ):
         for e in range(2):
-            ocopy(s, e, lambda z: z).wait_recv()
+            for pc in range(NC):
+                ocopy(s, e, pc, lambda z: z).wait_recv()
     o_ref[...] = obuf[...]
 
-    def sent(s, k):
-        dx, dy, dc = where_to(s)
-        dst = at(x + dx, y + dy, (c + dc) % NC)
-        kv_copy(dst, s).wait_send()
-        fill_copy(dst, s).wait_send()
-        return k
-
-    lax.fori_loop(1, GRP, sent, 0)
-
+    for d in kv_copies(sib, 0):
+        d.wait_send()
+
+    def sent(p, k, carry):
+        for d in give_to(p, k):
+            d.wait_send()
+        return carry
+
+    lax.fori_loop(EARLY + 1, CHIPS, functools.partial(sent, 0), 0)
+    lax.fori_loop(1, CHIPS, functools.partial(sent, 1), 0)
     for s in range(1, NZ):
         for e in range(2):
             zcopy(e, s, lambda z: t).wait_send()
-            ocopy(s, e, lambda z: t).wait_send()
-    for d in wsends + sends + shared:
-        d.wait_send()
+            for pc in range(NC):
+                ocopy(s, e, pc, lambda z: t).wait_send()
+    for n in range(NZ):
+        wsend(n).wait_send()
+    for h in range(2):
+        for d in ORDER:
+            share(h, *d).wait_send()
+            for p in pushes(h, *d):
+                p.wait_send()
 
 
 def body(queries, span_kv, cache, block_owner, block_fill, out_weight):
@@ -413,7 +490,7 @@
             dma((2, NZ)), dma((2, NZ)),
             dma((40,)), dma((GRP, 4)),
             dma((32,)), dma((GRP, 2)),
-            dma((NZ, 2)), dma((NZ, 2)),
+            dma((NZ, 2, NC)), dma((NZ, 2, NC)),
         ],
         compiler_params=pltpu.CompilerParams(
             collective_id=0, has_side_effects=True, vmem_limit_bytes=VMEM_LIMIT

time: 114 us -> 105 us (0.921)
  the two profiles are of different devices: /device:TPU:5 before, /device:TPU:1 now
where the time goes in v3:
time: 105 us; the launch traced here: 104 us
  Pallas kernels  103 us (98%)
  local copies, waits for them, and re-layouts  1.67 us (2%)
    pallas_call x1, Pallas kernels, body(): pl.pallas_call(main_kernel, out_shape=jax.ShapeDtypeStruct((GRP // NZ, NZ...  103 us

profile of v3, /device:TPU:1, one launch (start us, length us, event | category | flops | bytes accessed | tf_op | source)
XLA Modules:
  0.0 104.4 jit_solution(4181577427733777226)
XLA Ops:
  0.0 102.7 %shard_map.64 = bf16[4,8,16,256]{3,2,1,0:T(8,128)(2,1)} custom-call(s32[1,48]{1,0:T(1,128)} %bitcast.10, s32[1,48]{1,0:T(1,128)} %bitcast.11, bf16[128,1024]{1,0:T(8,128)(2,1)} %bitcast.8, bf16[128,256]{1,0:T(8,128)(2,1)} %bitcast.9, bf16[48,128,256]{2,1,0:T(8,128)(2,1)} %bitcast.6, bf16[1024,256]{1,0:T(8,128)(2,1)} %w_hbm.1), custom_call_target="tpu_custom_call" | custom-call | tf_op jit(solution)/shard_map/pallas_call | solution.py:461
  102.7 1.7 %copy.8 = bf16[512,256]{1,0:T(8,128)(2,1)} copy(bf16[512,256]{1,0:T(8,128)(2,1)} %bitcast.7) | data formatting | bytes 524288

commit v4 on v3

--- a/solution.py
+++ b/solution.py
@@ -267,9 +267,9 @@
         return at(x + d1, y + d2, pc) if h == 0 else at(x + d2, y + d1, pc)
 
     PUSHES = {
-        (0, 0): [((1, 0), 0, NZ, 0), ((3, 0), 0, NZ, 0), ((0, 1), 0, NZ, 0), ((0, 3), 0, NZ, 0)],
-        (3, 0): [((1, 0), 0, 4, 0), ((0, 1), 0, NZ, 0), ((0, 3), 0, NZ, 0)],
-        (1, 0): [((3, 0), 4, 4, 1), ((0, 1), 0, NZ, 0), ((0, 3), 0, NZ, 0)],
+        (0, 0): [((1, 0), 0, NZ, 0), ((3, 0), 0, NZ, 0), ((2, 0), 0, NZ, 0), ((0, 1), 0, NZ, 0), ((0, 3), 0, NZ, 0)],
+        (3, 0): [((0, 1), 0, NZ, 0), ((0, 3), 0, NZ, 0)],
+        (1, 0): [((0, 1), 0, NZ, 0), ((0, 3), 0, NZ, 0)],
         (2, 0): [((0, 1), 0, NZ, 0), ((0, 3), 0, NZ, 0)],
     }
     for d1 in range(4):
@@ -302,7 +302,7 @@
         lo = NZ * h
         q = 2 * h
         last = d2 if d2 else d1
-        if last == 2:
+        if d2 == 2:
             arrived(owner, lo, 4, q)
             arrived(owner, lo + 4, 4, q + 1)
         elif last:

time: 105 us -> 104 us (level)
  Pallas kernels: 103 us -> 101 us
    pallas_call x1, Pallas kernels: 103 us -> 101 us  [body(): pl.pallas_call(main_kernel, out_shape=jax.ShapeDtypeStruct((GRP // NZ, NZ...]
where the time goes in v4:
time: 104 us; the launch traced here: 103 us
  Pallas kernels  101 us (97%)
  local copies, waits for them, and re-layouts  1.67 us (2%)
    pallas_call x1, Pallas kernels, body(): pl.pallas_call(main_kernel, out_shape=jax.ShapeDtypeStruct((GRP // NZ, NZ...  101 us

profile of v4, /device:TPU:1, one launch (start us, length us, event | category | flops | bytes accessed | tf_op | source)
XLA Modules:
  0.0 103.0 jit_solution(9633129230183186254)
XLA Ops:
  0.0 101.3 %shard_map.64 = bf16[4,8,16,256]{3,2,1,0:T(8,128)(2,1)} custom-call(s32[1,48]{1,0:T(1,128)} %bitcast.10, s32[1,48]{1,0:T(1,128)} %bitcast.11, bf16[128,1024]{1,0:T(8,128)(2,1)} %bitcast.8, bf16[128,256]{1,0:T(8,128)(2,1)} %bitcast.9, bf16[48,128,256]{2,1,0:T(8,128)(2,1)} %bitcast.6, bf16[1024,256]{1,0:T(8,128)(2,1)} %w_hbm.1), custom_call_target="tpu_custom_call" | custom-call | tf_op jit(solution)/shard_map/pallas_call | solution.py:461
  101.3 1.7 %copy.8 = bf16[512,256]{1,0:T(8,128)(2,1)} copy(bf16[512,256]{1,0:T(8,128)(2,1)} %bitcast.7) | data formatting | bytes 524288

commit v5 on v4

--- a/solution.py
+++ b/solution.py
@@ -416,9 +416,10 @@
         multiply(0, near, 1)
         events(13, 14)
         multiply(1, near, 1)
-        events(14, 16)
+        events(14, 15)
         finish(1, False)
         for h in range(2):
+            event(h, *ORDER[15])
             multiply(h, (2,), 1)
 
     finish(1, True)

time: 104 us -> 104 us (level)
  no operation moved by 1% of the time
where the time goes in v5:
time: 104 us; the launch traced here: 103 us
  Pallas kernels  101 us (97%)
  local copies, waits for them, and re-layouts  1.67 us (2%)
    pallas_call x1, Pallas kernels, body(): pl.pallas_call(main_kernel, out_shape=jax.ShapeDtypeStruct((GRP // NZ, NZ...  101 us

profile of v5, /device:TPU:1, one launch (start us, length us, event | category | flops | bytes accessed | tf_op | source)
XLA Modules:
  0.0 103.1 jit_solution(13834112791048327171)
XLA Ops:
  0.0 101.4 %shard_map.64 = bf16[4,8,16,256]{3,2,1,0:T(8,128)(2,1)} custom-call(s32[1,48]{1,0:T(1,128)} %bitcast.10, s32[1,48]{1,0:T(1,128)} %bitcast.11, bf16[128,1024]{1,0:T(8,128)(2,1)} %bitcast.8, bf16[128,256]{1,0:T(8,128)(2,1)} %bitcast.9, bf16[48,128,256]{2,1,0:T(8,128)(2,1)} %bitcast.6, bf16[1024,256]{1,0:T(8,128)(2,1)} %w_hbm.1), custom_call_target="tpu_custom_call" | custom-call | tf_op jit(solution)/shard_map/pallas_call | solution.py:462
  101.4 1.7 %copy.8 = bf16[512,256]{1,0:T(8,128)(2,1)} copy(bf16[512,256]{1,0:T(8,128)(2,1)} %bitcast.7) | data formatting | bytes 524288
